TPU v7x, 512 devices: a whole 4x4x16 slice. The times are simulated.
512 devices in a mesh: dp: 64 (over y, z), feat: 8 (over x, core).
Axes of the slice: x: 4, y: 4, z: 16, core: 2. Of those that a mesh axis runs over, the one named last changes fastest.
Arguments:
- samples: bfloat16 [8192, 131072], P('dp', 'feat'), may hold values from -70 to 70
- estimates: bfloat16 [64, 8, 16384], P(None, 'feat', 'dp'), may hold values from -18 to 18
Outputs:
- updated: bfloat16 [64, 8, 16384], P(None, 'feat', 'dp')
All inputs are finite; a program needn't handle non-finite values.
Results may differ from a plain program's by a relative error of at most 0.0095.
Values may be sent and summed in bfloat16 or wider, within the bound.
A program may use at most 64 MiB of HBM per device.

v0:
```python
import math

import jax
import jax.numpy as jnp
from jax import lax
from jax.sharding import PartitionSpec as P

F = 131072


step_rate = 0.05
epsilon = 1e-06


def contract_last(left, right):
    return lax.dot_general(
        left, right, (((1,), (1,)), ((), ())), preferred_element_type=jnp.float32
    )


def shards(samples, estimates):
    components = estimates.shape[0]
    own_rows = estimates.shape[2]
    shaped = estimates.reshape(components, own_rows)
    total_samples = samples.shape[0] * lax.axis_size("dp")
    partial_value = contract_last(lax.all_gather(shaped, "dp", axis=1, tiled=True), samples)
    summed = lax.psum(partial_value.astype(jnp.bfloat16), "feat").astype(jnp.float32)
    scores = (summed * (1.0 / math.sqrt(F))).astype(jnp.bfloat16)
    gram_matrix = lax.psum(contract_last(scores, scores), "dp") / total_samples
    block_product = jnp.dot(scores, samples, preferred_element_type=jnp.float32)
    product = lax.psum_scatter(block_product, "dp", scatter_dimension=1, tiled=True)
    current = shaped.astype(jnp.float32)
    penalty = jnp.tril(gram_matrix, -1)
    update_dir = math.sqrt(F) / total_samples * product - jnp.dot(
        penalty, current, precision=lax.Precision.HIGHEST
    )
    alignment = lax.psum(jnp.sum(current * update_dir, axis=1), ("dp", "feat")) / F
    stepped = current + step_rate * (update_dir - alignment[:, None] * current)
    squares = lax.psum(jnp.sum(stepped * stepped, axis=1), ("dp", "feat")) / F
    updated = stepped * lax.rsqrt(squares + epsilon)[:, None]
    return updated.astype(jnp.bfloat16).reshape(components, 1, own_rows)


def solution(mesh):
    return jax.shard_map(
        shards,
        mesh=mesh,
        in_specs=(P("dp", "feat"), P(None, "feat", "dp")),
        out_specs=P(None, "feat", "dp"),
        check_vma=False,
    )
```

profile of v0, /device:TPU:1, one launch (start us, length us, event | category | flops | bytes accessed | tf_op | source)
XLA Modules:
  0.0 1088.5 jit_solution(3279829444135497381)
XLA Ops:
  6.5 0.0 all-gather.3.cloned.1.call-start
  6.5 0.7 all-gather.3.cloned.1.call-update
  7.3 0.0 reduce-scatter.2.cloned.1.call-start
  7.3 134.5 %all-gather.3.cloned.1.call-done = bf16[64,1,16384]{2,0,1:T(8,128)(2,1)} async-done(((bf16[64,1,256]{2,0,1:T(8,128)(2,1)}), bf16[64,1,16384]{2,0,1:T(8,128)(2,1)}) %all-gather.3.cloned.1.call-update) | async-done | bytes 2097168 | tf_op jit(solution)/shard_map/all_gather | solution.py:26
  141.8 4.4 fusion.2
  146.2 29.8 %psum.28 = bf16[64,128]{1,0:T(8,128)(2,1)S(1)} all-reduce(bf16[64,128]{1,0:T(8,128)(2,1)S(1)} %fusion.2), channel_id=1, replica_groups=mesh['dp'=64,'feat'=8] {'feat'}, use_global_device_ids=true, to_apply=%region_0.0 | all-reduce | flops 8192 | bytes 32768 | tf_op jit(solution)/shard_map/psum | solution.py:27
  176.0 4.8 fusion.16
  180.8 0.0 copy-start
  180.8 0.0 reduce-scatter.2.cloned.1.call-update
  180.9 0.1 fusion.15
  181.0 223.1 %psum.29 = f32[64,64]{1,0:T(8,128)S(1)} all-reduce(f32[64,64]{1,0:T(8,128)S(1)} %fusion.15), channel_id=1, replica_groups=mesh['dp'=64,'feat'=8] {'dp'}, use_global_device_ids=true, to_apply=%region_2.0 | all-reduce | flops 4096 | bytes 32768 | tf_op jit(solution)/shard_map/psum | solution.py:29
  404.1 463.1 %reduce-scatter.2.cloned.1.call-done = f32[64,256]{1,0:T(8,128)} async-done(((f32[64,16384]{1,0:T(8,128)}), f32[64,256]{1,0:T(8,128)}) %reduce-scatter.2.cloned.1.call-update) | async-done | bytes 65552 | tf_op jit(solution)/shard_map/reduce_scatter | solution.py:31
  867.3 0.0 copy-done
  867.3 1.2 fusion.5
  868.4 113.0 %psum.30 = f32[64]{0:T(128)S(1)} all-reduce(f32[64]{0:T(128)S(1)} %get-tuple-element.5), channel_id=1, replica_groups=mesh['dp'=64,'feat'=8] {'dp','feat'}, use_global_device_ids=true, to_apply=%region_4.5 | all-reduce | flops 64 | bytes 512 | tf_op jit(solution)/shard_map/psum | solution.py:37
  981.4 0.2 multiply_reduce_fusion
  981.6 99.3 %psum.31 = f32[64]{0:T(128)S(1)} all-reduce(f32[64]{0:T(128)S(1)} %multiply_reduce_fusion), channel_id=1, replica_groups=mesh['dp'=64,'feat'=8] {'dp','feat'}, use_global_device_ids=true, to_apply=%region_6.7 | all-reduce | flops 64 | bytes 512 | tf_op jit(solution)/shard_map/psum | solution.py:39
  1080.9 0.7 fusion.8
  (3 shorter events, 0.0 us)
Async XLA Ops:
  6.5 135.3 %all-gather.3.cloned.1.call-start = ((), (), s32[]{:S(2)}) async-start(), calls=%async_computation.2 | async-start | bytes 2129920 | tf_op jit(solution)/shard_map/all_gather | solution.py:26
  7.3 860.0 %reduce-scatter.2.cloned.1.call-start = ((), (), s32[]{:S(2)}) async-start(), calls=%async_computation.1 | async-start | bytes 4259840 | tf_op jit(solution)/shard_map/reduce_scatter | solution.py:31
  180.8 686.4 %copy-start = (bf16[64,1,256]{2,0,1:T(8,128)(2,1)S(1)}, bf16[64,1,256]{2,0,1:T(8,128)(2,1)}, u32[]{:S(2)}) copy-start(bf16[64,1,256]{2,0,1:T(8,128)(2,1)} %param.3) | copy-start | bytes 98308
Sparse Core Ops, SparseCore 0:
  10.3 131.5 all-gather.2
  181.0 686.2 reduce-scatter.1
where the time goes:
time: 1090 us
  waiting for transfers between devices  598 us (55%)
  blocking collectives  465 us (43%)
  between operations  13.4 us (1%)
    reduce_scatter x1, waiting for transfers between devices, shards(): lax.psum_scatter(block_product, 'dp', scatter_dimension=1, tiled=True)  463 us
    psum x1, blocking collectives, shards(): gram_matrix = lax.psum(contract_last(scores, scores), 'dp') / total_samples  223 us
    all_gather x1, waiting for transfers between devices, shards(): lax.all_gather(shaped, 'dp', axis=1, tiled=True)  135 us
    psum x1, blocking collectives, shards(): lax.psum(jnp.sum(current * update_dir, axis=1), ('dp', 'feat')) / F  113 us
    psum x1, blocking collectives, shards(): squares = lax.psum(jnp.sum(stepped * stepped, axis=1), ('dp', 'feat')) / F  99.3 us
    psum x1, blocking collectives, shards(): lax.psum(partial_value.astype(jnp.bfloat16), 'feat').astype(jnp.float32)  29.8 us
  transfers between devices with their start and end apart: 2, of which 2 were waited for; matrix products, arithmetic and copies ran while one was open for 0% of the time, Pallas kernels for 0%

commit v1 on v0

v1 whole, which is shorter than its diff:
```python
import functools
import math

import jax
import jax.numpy as jnp
from jax import lax
from jax.experimental import pallas as pl
from jax.experimental.pallas import tpu as pltpu
from jax.sharding import PartitionSpec as P

F = 131072
STEP = 0.05
EPSILON = 1e-06
MESH = pl.DeviceIdType.MESH

NY, NZ, NF = 4, 16, 8
K = 64
ROWS = 128
WIDTH = 256
HALF = NZ // 2


def kernel(
    total_samples,
    x_hbm,
    u_ref,
    o_ref,
    x_v,
    gathered,
    score_slots,
    y_out,
    y_in,
    chain_out,
    chain_in,
    across_out,
    across_in,
    stat_z,
    stat_y,
    stat_f,
    x_sem,
    gather_send,
    gather_recv,
    score_send,
    score_recv,
    scatter_send,
    y_recv,
    chain_recv,
    across_recv,
    stat_send,
    stat_recv,
):
    dp = lax.axis_index("dp")
    feat = lax.axis_index("feat")
    y = dp // NZ
    z = dp % NZ
    up, down, across = (y + 1) % NY, (y + NY - 1) % NY, (y + 2) % NY

    def zof(offset):
        return (z + offset + NZ) % NZ

    right, left = zof(1), zof(-1)

    x_copy = pltpu.make_async_copy(x_hbm, x_v, x_sem)
    x_copy.start()

    barrier = pltpu.get_barrier_semaphore()
    partners = (
        [(dp // NZ * NZ + zof(i), feat) for i in range(1, NZ)]
        + [((y + i) % NY * NZ + z, feat) for i in range(1, NY)]
        + [(dp, (feat + i) % NF) for i in range(1, NF)]
    )
    for partner in partners:
        pl.semaphore_signal(barrier, inc=1, device_id=partner, device_id_type=MESH)
    pl.semaphore_wait(barrier, len(partners))

    def gather_copy(row, plane, to_row, to_plane, src=None):
        index = row * NZ + plane
        return pltpu.make_async_remote_copy(
            src_ref=gathered.at[index] if src is None else src,
            dst_ref=gathered.at[index],
            send_sem=gather_send,
            recv_sem=gather_recv.at[index],
            device_id=(to_row * NZ + to_plane, feat),
            device_id_type=MESH,
        )

    def arrived(row, plane):
        gather_copy(row, plane, y, right).wait_recv()

    for to_row, to_plane in ((y, right), (y, left), (across, z), (up, z), (down, z)):
        gather_copy(y, z, to_row, to_plane, u_ref).start()
    gathered[dp] = u_ref[...]

    def partial_scores(acc, row, plane):
        index = row * NZ + plane
        columns = pl.ds(pl.multiple_of(index * WIDTH, WIDTH), WIDTH)
        return acc + lax.dot_general(
            gathered[index],
            x_v[:, columns],
            (((1,), (1,)), ((), ())),
            preferred_element_type=jnp.float32,
        )

    arrived(across, z)
    gather_copy(across, z, y, right).start()
    gather_copy(across, z, y, left).start()
    x_copy.wait()
    acc = jnp.zeros((K, ROWS), jnp.float32)
    acc = partial_scores(acc, y, z)
    acc = partial_scores(acc, across, z)

    def gather_step(hop, acc, near, far_in, far_out):
        behind, ahead = zof(-hop), zof(hop)
        arrived(y, behind)
        if far_out:
            gather_copy(y, behind, y, right).start()
        gather_copy(y, behind, up, z).start()
        gather_copy(y, behind, down, z).start()
        arrived(across, ahead)
        if far_out:
            gather_copy(across, ahead, y, left).start()
        if near:
            arrived(y, ahead)
            if far_in:
                gather_copy(y, ahead, y, left).start()
            gather_copy(y, ahead, up, z).start()
            gather_copy(y, ahead, down, z).start()
            arrived(across, behind)
            if far_in:
                gather_copy(across, behind, y, right).start()
        acc = partial_scores(acc, y, behind)
        acc = partial_scores(acc, across, ahead)
        if near:
            acc = partial_scores(acc, y, ahead)
            acc = partial_scores(acc, across, behind)
        return acc

    def side_rows(acc, planes):
        for plane in planes:
            for row in (up, down):
                arrived(row, plane)
                acc = partial_scores(acc, row, plane)
        return acc

    acc = gather_step(1, acc, True, True, True)
    acc = side_rows(acc, (z,))

    def middle(hop, acc):
        acc = gather_step(hop, acc, True, True, True)
        return side_rows(acc, (zof(1 - hop), zof(hop - 1)))

    acc = lax.fori_loop(2, HALF - 1, middle, acc)
    acc = gather_step(HALF - 1, acc, True, False, True)
    acc = side_rows(acc, (zof(2 - HALF), zof(HALF - 2)))
    acc = gather_step(HALF, acc, False, False, False)
    acc = side_rows(acc, (zof(1 - HALF), zof(HALF - 1), zof(HALF)))

    score_slots[feat] = acc.astype(jnp.bfloat16)

    def score_copy(i):
        return pltpu.make_async_remote_copy(
            src_ref=score_slots.at[feat],
            dst_ref=score_slots.at[feat],
            send_sem=score_send,
            recv_sem=score_recv,
            device_id=(dp, (feat + i) % NF),
            device_id_type=MESH,
        )

    for i in range(1, NF):
        score_copy(i).start()
    seven = score_slots.at[pl.ds(0, NF - 1)]
    pltpu.make_async_copy(seven, seven, score_recv).wait()
    summed = score_slots[0].astype(jnp.float32)
    for i in range(1, NF):
        summed = summed + score_slots[i].astype(jnp.float32)
    scores = (summed * (1.0 / math.sqrt(F))).astype(jnp.bfloat16)

    gram = lax.dot_general(
        scores, scores, (((1,), (1,)), ((), ())), preferred_element_type=jnp.float32
    )
    below = lax.broadcasted_iota(jnp.int32, (K, K), 0) > lax.broadcasted_iota(
        jnp.int32, (K, K), 1
    )
    penalty = jnp.where(below, gram * (-1.0 / math.sqrt(F)), 0.0)
    high = penalty.astype(jnp.bfloat16)
    low = (penalty - high.astype(jnp.float32)).astype(jnp.bfloat16)
    weights = jnp.concatenate([scores, high, low], axis=1)

    def term(row, plane):
        index = row * NZ + plane
        columns = pl.ds(pl.multiple_of(index * WIDTH, WIDTH), WIDTH)
        shard = gathered[index]
        return jnp.dot(
            weights,
            jnp.concatenate([x_v[:, columns], shard, shard], axis=0),
            preferred_element_type=jnp.float32,
        )

    def side_copy(side, plane, to_row):
        return pltpu.make_async_remote_copy(
            src_ref=y_out.at[side, plane],
            dst_ref=y_in.at[side, plane],
            send_sem=scatter_send,
            recv_sem=y_recv.at[side, plane],
            device_id=(to_row * NZ + z, feat),
            device_id_type=MESH,
        )

    def send_sides(planes):
        for plane in planes:
            for side, row in ((0, up), (1, down)):
                y_out[side, plane] = term(row, plane).astype(jnp.bfloat16)
                side_copy(side, plane, row).start()

    def take_sides(total, plane):
        for side in (0, 1):
            side_copy(side, plane, up).wait_recv()
            total = total + y_in[side, plane].astype(jnp.float32)
        return total

    def chain_copy(lane, hop):
        return pltpu.make_async_remote_copy(
            src_ref=chain_out.at[lane, hop - 1],
            dst_ref=chain_in.at[lane, hop - 1],
            send_sem=scatter_send,
            recv_sem=chain_recv.at[lane, hop - 1],
            device_id=(y * NZ + (left if lane in (0, 3) else right), feat),
            device_id_type=MESH,
        )

    def take_chain(total, lane, hop):
        chain_copy(lane, hop + 1).wait_recv()
        return total + chain_in[lane, hop].astype(jnp.float32)

    def send_chain(total, lane, hop):
        chain_out[lane, hop - 1] = total.astype(jnp.bfloat16)
        chain_copy(lane, hop).start()

    def scatter_step(hop, lanes, heads, next_planes):
        behind, ahead = zof(-hop), zof(hop)
        send_sides(next_planes)
        where = {0: (y, behind), 1: (across, ahead), 2: (y, ahead), 3: (across, behind)}
        totals = {lane: term(*where[lane]) for lane in lanes}
        for lane in lanes:
            total = totals[lane]
            if lane in (0, 2):
                total = take_sides(total, where[lane][1])
            if lane not in heads:
                total = take_chain(total, lane, hop)
            send_chain(total, lane, hop)

    send_sides((zof(HALF),))
    scatter_step(HALF, (1, 0), (1, 0), (zof(1 - HALF), zof(HALF - 1)))
    scatter_step(HALF - 1, (1, 3, 0, 2), (3, 2), (zof(2 - HALF), zof(HALF - 2)))

    @pl.loop(0, HALF - 3)
    def _(i):
        hop = HALF - 2 - i
        scatter_step(hop, (1, 3, 0, 2), (), (zof(1 - hop), zof(hop - 1)))

    scatter_step(1, (1, 3, 0, 2), (), (z,))

    across_copy = pltpu.make_async_remote_copy(
        src_ref=across_out,
        dst_ref=across_in,
        send_sem=scatter_send,
        recv_sem=across_recv,
        device_id=(across * NZ + z, feat),
        device_id_type=MESH,
    )
    opposite = term(across, z)
    own = term(y, z)
    opposite = take_chain(take_chain(opposite, 1, 0), 3, 0)
    across_out[...] = opposite.astype(jnp.bfloat16)
    across_copy.start()
    own = take_sides(own, z)
    own = take_chain(take_chain(own, 0, 0), 2, 0)
    across_copy.wait_recv()
    own = own + across_in[...].astype(jnp.float32)

    current = u_ref[...].astype(jnp.float32)
    update = own * (math.sqrt(F) / total_samples)
    lane_of = lax.broadcasted_iota(jnp.int32, (K, 128), 1)
    stats = jnp.zeros((K, 128), jnp.float32)
    for lane, value in enumerate((current * current, current * update, update * update)):
        column = jnp.sum(value, axis=1, keepdims=True)
        stats = jnp.where(lane_of == lane, column, stats)
    stats = jnp.concatenate([stats, jnp.zeros_like(stats)], axis=0).T[:8]

    def total_over(stage, slots, me, count, device_of, value):
        slots[me] = value
        for i in range(1, count):
            pltpu.make_async_remote_copy(
                src_ref=slots.at[me],
                dst_ref=slots.at[me],
                send_sem=stat_send.at[stage],
                recv_sem=stat_recv.at[stage],
                device_id=device_of(i),
                device_id_type=MESH,
            ).start()
        others = slots.at[pl.ds(0, count - 1)]
        pltpu.make_async_copy(others, others, stat_recv.at[stage]).wait()
        total = slots[0]
        for i in range(1, count):
            total = total + slots[i]
        return total

    stats = total_over(0, stat_z, z, NZ, lambda i: (y * NZ + zof(i), feat), stats)
    stats = total_over(1, stat_y, y, NY, lambda i: ((y + i) % NY * NZ + z, feat), stats)
    stats = total_over(2, stat_f, feat, NF, lambda i: (dp, (feat + i) % NF), stats)

    columns = jnp.concatenate([stats, jnp.zeros((120, 128), jnp.float32)], axis=0).T[:K]
    columns = columns * (1.0 / F)
    alignment = columns[:, 1:2]
    keep = 1.0 - STEP * alignment
    squares = (
        keep * keep * columns[:, 0:1]
        + 2.0 * STEP * keep * alignment
        + STEP * STEP * columns[:, 2:3]
    )
    scale = lax.rsqrt(jnp.maximum(squares, 0.0) + EPSILON)
    o_ref[...] = ((keep * current + STEP * update) * scale).astype(jnp.bfloat16)

    sent = gathered.at[pl.ds(0, NY * NZ - 1)]
    pltpu.make_async_copy(sent, sent, gather_send).wait()
    pltpu.make_async_copy(seven, seven, score_send).wait()
    pltpu.make_async_copy(sent, sent, scatter_send).wait()
    for stage, (slots, count) in enumerate(((stat_z, NZ), (stat_y, NY), (stat_f, NF))):
        others = slots.at[pl.ds(0, count - 1)]
        pltpu.make_async_copy(others, others, stat_send.at[stage]).wait()


def shards(samples, estimates):
    shaped = estimates.reshape(K, WIDTH)
    total_samples = samples.shape[0] * lax.axis_size("dp")
    bf16, f32 = jnp.bfloat16, jnp.float32
    dma = pltpu.SemaphoreType.DMA
    updated = pl.pallas_call(
        functools.partial(kernel, total_samples),
        out_shape=jax.ShapeDtypeStruct((K, WIDTH), bf16),
        in_specs=[
            pl.BlockSpec(memory_space=pl.ANY),
            pl.BlockSpec(memory_space=pltpu.VMEM),
        ],
        out_specs=pl.BlockSpec(memory_space=pltpu.VMEM),
        scratch_shapes=[
            pltpu.VMEM((ROWS, NY * NZ * WIDTH), bf16),
            pltpu.VMEM((NY * NZ, K, WIDTH), bf16),
            pltpu.VMEM((NF, K, ROWS), bf16),
            pltpu.VMEM((2, NZ, K, WIDTH), bf16),
            pltpu.VMEM((2, NZ, K, WIDTH), bf16),
            pltpu.VMEM((4, HALF, K, WIDTH), bf16),
            pltpu.VMEM((4, HALF, K, WIDTH), bf16),
            pltpu.VMEM((K, WIDTH), bf16),
            pltpu.VMEM((K, WIDTH), bf16),
            pltpu.VMEM((NZ, 8, 128), f32),
            pltpu.VMEM((NY, 8, 128), f32),
            pltpu.VMEM((NF, 8, 128), f32),
            dma,
            dma,
            dma((NY * NZ,)),
            dma,
            dma,
            dma,
            dma((2, NZ)),
            dma((4, HALF)),
            dma,
            dma((3,)),
            dma((3,)),
        ],
        compiler_params=pltpu.CompilerParams(
            collective_id=0,
            has_side_effects=True,
            vmem_limit_bytes=48 * 1024 * 1024,
        ),
        cost_estimate=pl.CostEstimate(
            flops=4 * K * ROWS * NY * NZ * WIDTH,
            bytes_accessed=2 * ROWS * NY * NZ * WIDTH,
            transcendentals=0,
        ),
    )(samples, shaped)
    return updated.reshape(K, 1, WIDTH)


def solution(mesh):
    return jax.shard_map(
        shards,
        mesh=mesh,
        in_specs=(P("dp", "feat"), P(None, "feat", "dp")),
        out_specs=P(None, "feat", "dp"),
        check_vma=False,
    )
```

time: 1090 us -> 106 us (0.10)
  waiting for transfers between devices: 598 us -> 0 us
  blocking collectives: 465 us -> 0 us
  Pallas kernels: 0 us -> 102 us
  between operations: 13.4 us -> 0.01 us
    psum x4 -> x0, blocking collectives: 465 us -> none  [the longest x1 223 us: shards(): gram_matrix = lax.psum(contract_last(scores, scores), 'dp') / total_samples]
    reduce_scatter x1 -> x0, waiting for transfers between devices: 463 us -> none  [shards(): lax.psum_scatter(block_product, 'dp', scatter_dimension=1, tiled=True)]
    all_gather x1 -> x0, waiting for transfers between devices: 135 us -> none  [shards(): lax.all_gather(shaped, 'dp', axis=1, tiled=True)]
    pallas_call x0 -> x1, Pallas kernels: none -> 102 us  [shards(): pl.pallas_call(functools.partial(kernel, total_samples), out_shape=jax.Sh...]
  transfers between devices with their start and end apart: 2 -> 0, of which waited for: 2 -> 0; matrix products, arithmetic and copies ran while one was open for 0% -> 0% of each run, Pallas kernels for 0% -> 0%
where the time goes in v1:
time: 106 us
  Pallas kernels  102 us (96%)
  local copies, waits for them, and re-layouts  3.56 us (3%)
    pallas_call x1, Pallas kernels, shards(): pl.pallas_call(functools.partial(kernel, total_samples), out_shape=jax.Sh...  102 us
    unnamed x5, local copies, waits for them, and re-layouts  3.56 us

profile of v1, /device:TPU:1, one launch (start us, length us, event | category | flops | bytes accessed | tf_op | source)
XLA Modules:
  0.0 105.7 jit_solution(13573609511246453338)
XLA Ops:
  0.0 0.0 copy-start
  0.0 2.2 %copy-done = bf16[128,16384]{1,0:T(8,128)(2,1)S(1)} copy-done((bf16[128,16384]{1,0:T(8,128)(2,1)S(1)}, bf16[128,16384]{1,0:T(8,128)(2,1)}, u32[]{:S(2)}) %copy-start) | copy-done | bytes 4194328
  2.2 0.0 copy-start.1
  2.2 0.8 copy-done.1
  2.9 102.1 %shard_map.28 = bf16[64,256]{1,0:T(8,128)(2,1)S(1)} custom-call(bf16[128,16384]{1,0:T(8,128)(2,1)S(1)} %copy-done, bf16[64,256]{1,0:T(8,128)(2,1)S(1)} %bitcast.3), custom_call_target="tpu_custom_call" | custom-call | flops 536870912 | bytes 4194304 | tf_op jit(solution)/shard_map/pallas_call | solution.py:339
  105.1 0.6 copy.4
Async XLA Ops:
  0.0 2.2 %copy-start = (bf16[128,16384]{1,0:T(8,128)(2,1)S(1)}, bf16[128,16384]{1,0:T(8,128)(2,1)}, u32[]{:S(2)}) copy-start(bf16[128,16384]{1,0:T(8,128)(2,1)} %x_hbm.1) | copy-start | bytes 12582916
  2.2 0.8 copy-start.1

commit v2 on v1

--- a/solution.py
+++ b/solution.py
@@ -23,9 +23,10 @@
 def kernel(
     total_samples,
     x_hbm,
-    u_ref,
+    u_hbm,
     o_ref,
     x_v,
+    u_ref,
     gathered,
     score_slots,
     y_out,
@@ -38,6 +39,7 @@
     stat_y,
     stat_f,
     x_sem,
+    u_sem,
     gather_send,
     gather_recv,
     score_send,
@@ -61,16 +63,19 @@
     right, left = zof(1), zof(-1)
 
     x_copy = pltpu.make_async_copy(x_hbm, x_v, x_sem)
+    u_copy = pltpu.make_async_copy(u_hbm, u_ref, u_sem)
+    u_copy.start()
     x_copy.start()
 
     barrier = pltpu.get_barrier_semaphore()
     partners = (
-        [(dp // NZ * NZ + zof(i), feat) for i in range(1, NZ)]
+        [(y * NZ + right, feat), (y * NZ + left, feat)]
         + [((y + i) % NY * NZ + z, feat) for i in range(1, NY)]
         + [(dp, (feat + i) % NF) for i in range(1, NF)]
     )
     for partner in partners:
         pl.semaphore_signal(barrier, inc=1, device_id=partner, device_id_type=MESH)
+    u_copy.wait()
     pl.semaphore_wait(barrier, len(partners))
 
     def gather_copy(row, plane, to_row, to_plane, src=None):
@@ -290,7 +295,7 @@
 
     def total_over(stage, slots, me, count, device_of, value):
         slots[me] = value
-        for i in range(1, count):
+        for i in sorted(range(1, count), key=lambda i: -min(i, count - i)):
             pltpu.make_async_remote_copy(
                 src_ref=slots.at[me],
                 dst_ref=slots.at[me],
@@ -341,11 +346,12 @@
         out_shape=jax.ShapeDtypeStruct((K, WIDTH), bf16),
         in_specs=[
             pl.BlockSpec(memory_space=pl.ANY),
-            pl.BlockSpec(memory_space=pltpu.VMEM),
+            pl.BlockSpec(memory_space=pl.ANY),
         ],
         out_specs=pl.BlockSpec(memory_space=pltpu.VMEM),
         scratch_shapes=[
             pltpu.VMEM((ROWS, NY * NZ * WIDTH), bf16),
+            pltpu.VMEM((K, WIDTH), bf16),
             pltpu.VMEM((NY * NZ, K, WIDTH), bf16),
             pltpu.VMEM((NF, K, ROWS), bf16),
             pltpu.VMEM((2, NZ, K, WIDTH), bf16),
@@ -359,6 +365,7 @@
             pltpu.VMEM((NF, 8, 128), f32),
             dma,
             dma,
+            dma,
             dma((NY * NZ,)),
             dma,
             dma,
@@ -372,7 +379,7 @@
         compiler_params=pltpu.CompilerParams(
             collective_id=0,
             has_side_effects=True,
-            vmem_limit_bytes=48 * 1024 * 1024,
+            vmem_limit_bytes=60 * 1024 * 1024,
         ),
         cost_estimate=pl.CostEstimate(
             flops=4 * K * ROWS * NY * NZ * WIDTH,

time: 106 us -> 100 us (0.943)
  Pallas kernels: 102 us -> 98.9 us
  local copies, waits for them, and re-layouts: 3.56 us -> 1.38 us
    pallas_call x1, Pallas kernels: 102 us -> 98.9 us  [shards(): pl.pallas_call(functools.partial(kernel, total_samples), out_shape=jax.Sh...]
    unnamed x5 -> x1, local copies, waits for them, and re-layouts: 3.56 us -> 1.38 us
where the time goes in v2:
time: 100 us
  Pallas kernels  98.9 us (99%)
  local copies, waits for them, and re-layouts  1.38 us (1%)
    pallas_call x1, Pallas kernels, shards(): pl.pallas_call(functools.partial(kernel, total_samples), out_shape=jax.Sh...  98.9 us

profile of v2, /device:TPU:1, one launch (start us, length us, event | category | flops | bytes accessed | tf_op | source)
XLA Modules:
  0.0 100.2 jit_solution(5552006633155480351)
XLA Ops:
  0.0 98.9 %shard_map.28 = bf16[64,256]{1,0:T(8,128)(2,1)} custom-call(bf16[128,16384]{1,0:T(8,128)(2,1)} %x_hbm.1, bf16[64,256]{1,0:T(8,128)(2,1)} %bitcast.3), custom_call_target="tpu_custom_call" | custom-call | flops 536870912 | bytes 4194304 | tf_op jit(solution)/shard_map/pallas_call | solution.py:344
  98.9 1.4 %copy.4 = bf16[64,1,256]{2,0,1:T(8,128)(2,1)} copy(bf16[64,1,256]{2,0,1:T(8,128)(2,1)} %bitcast.2) | data formatting | bytes 65536

commit v3 on v2

v3 whole, which is shorter than its diff:
```python
import functools
import math

import jax
import jax.numpy as jnp
from jax import lax
from jax.experimental import pallas as pl
from jax.experimental.pallas import tpu as pltpu
from jax.sharding import PartitionSpec as P

F = 131072
STEP = 0.05
EPSILON = 1e-06
MESH = pl.DeviceIdType.MESH
GROUP = 2
AHEAD = 2
ROOT = (0, 0)

NY, NZ, NF = 4, 16, 8
K = 64
ROWS = 128
WIDTH = 256

ARRIVALS = (
    (-1, 0), (1, 0), (0, 3), (0, -3), (2, 0), (0, 1), (0, -1), (-1, 1),
    (-1, -1), (1, -1), (-1, 3), (1, 3), (-1, -3), (1, -3), (0, 6), (2, 1),
    (1, 1), (0, -6), (0, 4), (2, -1), (0, -4), (0, -2), (2, 3), (-1, -2),
    (2, -3), (-1, 4), (-1, 2), (1, -2), (-1, -6), (2, 6), (0, 5), (0, 7),
    (-1, -4), (1, 6), (0, -7), (1, 2), (2, -2), (1, -6), (2, -4), (0, -5),
    (2, 2), (1, 4), (-1, -7), (2, 7), (2, -6), (0, 2), (2, 5), (1, 7),
    (-1, 5), (-1, 6), (0, 8), (1, -5), (1, -4), (1, -7), (2, -5), (-1, -5),
    (2, 4), (2, 8), (-1, 8), (1, 5), (-1, 7), (1, 8), (2, -7),
)
TARGETS = {
    (0, 0): ((0, 3), (0, -3), (-1, 0), (0, 1), (1, 0), (2, 0), (0, -1)),
    (-1, 0): ((-1, -1), (-1, 1)),
    (1, 0): ((1, -1),),
    (0, 3): ((0, 6), (0, 4), (-1, 3), (1, 3)),
    (0, -3): ((0, -6), (-1, -3), (0, -4), (1, -3), (0, -2)),
    (0, 1): ((1, 1),),
    (-1, 1): ((2, 1),),
    (-1, -1): ((-1, -2), (2, -1)),
    (-1, 3): ((-1, 2), (-1, 4)),
    (1, 3): ((2, 3),),
    (-1, -3): ((2, -3),),
    (1, -3): ((1, -2),),
    (0, 6): ((2, 6), (1, 6), (0, 5), (0, 7)),
    (1, 1): ((1, 2),),
    (0, -6): ((-1, -6), (0, -5), (0, -7), (1, -6)),
    (0, 4): ((1, 4),),
    (0, -4): ((-1, -4),),
    (-1, -2): ((2, -2),),
    (2, -3): ((2, -4),),
    (-1, 2): ((0, 2), (2, 2)),
    (-1, -6): ((2, -6), (-1, -7)),
    (2, 6): ((2, 5), (2, 7), (-1, 6)),
    (0, 5): ((-1, 5),),
    (1, 6): ((1, 7),),
    (0, -7): ((0, 8), (1, -7)),
    (1, -6): ((1, -5),),
    (2, -4): ((2, -5), (1, -4)),
    (0, -5): ((-1, -5),),
    (1, 4): ((2, 4),),
    (-1, -7): ((-1, 8),),
    (2, 7): ((2, 8), (-1, 7)),
    (2, -6): ((2, -7),),
    (2, 5): ((1, 5),),
    (1, 7): ((1, 8),),
}
NUMBER = {node: i for i, node in enumerate(ARRIVALS)}
COPIES = len(ARRIVALS)


def minus(a, b):
    dy, dz = (a[0] - b[0]) % NY, (a[1] - b[1]) % NZ
    return dy if dy <= NY // 2 else dy - NY, dz if dz <= NZ // 2 else dz - NZ


MOVES = sorted(
    {
        way
        for node, targets in TARGETS.items()
        for target in targets
        for way in (minus(target, node), minus(node, target))
    }
)


def kernel(
    total_samples,
    x_hbm,
    u_hbm,
    o_ref,
    x_v,
    u_ref,
    gathered,
    score_slots,
    scatter_out,
    scatter_in,
    stat_z,
    stat_y,
    stat_f,
    x_sem,
    u_sem,
    gather_send,
    gather_recv,
    score_send,
    score_recv,
    scatter_send,
    scatter_recv,
    stat_send,
    stat_recv,
):
    dp = lax.axis_index("dp")
    feat = lax.axis_index("feat")
    y = lax.div(dp, NZ)
    z = lax.rem(dp, NZ)

    def peer(dy, dz):
        return lax.rem(y + (dy + NY), NY) * NZ + lax.rem(z + (dz + NZ), NZ)

    def origin(node):
        return peer(-node[0], -node[1])

    def feat_peer(i):
        return lax.rem(feat + i, NF)

    x_copy = pltpu.make_async_copy(x_hbm, x_v, x_sem)
    u_copy = pltpu.make_async_copy(u_hbm, u_ref, u_sem)
    u_copy.start()
    x_copy.start()

    barrier = pltpu.get_barrier_semaphore()
    partners = [(peer(*way), feat) for way in MOVES]
    partners += [(dp, feat_peer(i)) for i in range(1, NF)]
    for partner in partners:
        pl.semaphore_signal(barrier, inc=1, device_id=partner, device_id_type=MESH)
    u_copy.wait()
    pl.semaphore_wait(barrier, len(partners))

    def gather_copy(node, target, src=None):
        index = origin(node)
        return pltpu.make_async_remote_copy(
            src_ref=gathered.at[index] if src is None else src,
            dst_ref=gathered.at[index],
            send_sem=gather_send,
            recv_sem=gather_recv.at[NUMBER[target]],
            device_id=(peer(*minus(target, node)), feat),
            device_id_type=MESH,
        )

    def arrived(node):
        shard = gathered.at[origin(node)]
        pltpu.make_async_copy(shard, shard, gather_recv.at[NUMBER[node]]).wait()

    for target in TARGETS[ROOT]:
        gather_copy(ROOT, target, u_ref).start()
    gathered[dp] = u_ref[...]

    def columns_of(index):
        return pl.ds(pl.multiple_of(index * WIDTH, WIDTH), WIDTH)

    def partial_scores(acc, nodes):
        for node in nodes:
            index = origin(node)
            acc = acc + lax.dot_general(
                gathered[index],
                x_v[:, columns_of(index)],
                (((1,), (1,)), ((), ())),
                preferred_element_type=jnp.float32,
            )
        return acc

    x_copy.wait()
    acc = partial_scores(jnp.zeros((K, ROWS), jnp.float32), (ROOT,))
    for start in range(0, COPIES, GROUP):
        group = ARRIVALS[start : start + GROUP]
        for node in group:
            arrived(node)
            for target in TARGETS.get(node, ()):
                gather_copy(node, target).start()
        acc = partial_scores(acc, group)

    score_slots[feat] = acc.astype(jnp.bfloat16)

    def score_copy(i):
        return pltpu.make_async_remote_copy(
            src_ref=score_slots.at[feat],
            dst_ref=score_slots.at[feat],
            send_sem=score_send,
            recv_sem=score_recv,
            device_id=(dp, feat_peer(i)),
            device_id_type=MESH,
        )

    for i in range(1, NF):
        score_copy(i).start()
    seven = score_slots.at[pl.ds(0, NF - 1)]
    pltpu.make_async_copy(seven, seven, score_recv).wait()
    summed = score_slots[0].astype(jnp.float32)
    for i in range(1, NF):
        summed = summed + score_slots[i].astype(jnp.float32)
    scores = (summed * (1.0 / math.sqrt(F))).astype(jnp.bfloat16)

    gram = lax.dot_general(
        scores, scores, (((1,), (1,)), ((), ())), preferred_element_type=jnp.float32
    )
    below = lax.broadcasted_iota(jnp.int32, (K, K), 0) > lax.broadcasted_iota(
        jnp.int32, (K, K), 1
    )
    penalty = jnp.where(below, gram * (-1.0 / math.sqrt(F)), 0.0)
    high = penalty.astype(jnp.bfloat16)
    low = (penalty - high.astype(jnp.float32)).astype(jnp.bfloat16)
    weights = jnp.concatenate([scores, high, low], axis=1)

    def term(node):
        index = origin(node)
        shard = gathered[index]
        return jnp.dot(
            weights,
            jnp.concatenate([x_v[:, columns_of(index)], shard, shard], axis=0),
            preferred_element_type=jnp.float32,
        )

    def scatter_copy(node, target):
        slot = NUMBER[target]
        return pltpu.make_async_remote_copy(
            src_ref=scatter_out.at[slot],
            dst_ref=scatter_in.at[slot],
            send_sem=scatter_send,
            recv_sem=scatter_recv.at[slot],
            device_id=(peer(*minus(node, target)), feat),
            device_id_type=MESH,
        )

    def take(total, node):
        for target in reversed(TARGETS.get(node, ())):
            slot = NUMBER[target]
            pltpu.make_async_copy(
                scatter_in.at[slot], scatter_in.at[slot], scatter_recv.at[slot]
            ).wait()
            total = total + scatter_in[slot].astype(jnp.float32)
        return total

    sources = {target: node for node, targets in TARGETS.items() for target in targets}
    departures = ARRIVALS[::-1] + (ROOT,)
    terms = [term(node) for node in departures[:AHEAD]]
    for i, node in enumerate(departures):
        if i + AHEAD < len(departures):
            terms.append(term(departures[i + AHEAD]))
        total = take(terms.pop(0), node)
        if node != ROOT:
            scatter_out[NUMBER[node]] = total.astype(jnp.bfloat16)
            scatter_copy(sources[node], node).start()
    own = total

    current = u_ref[...].astype(jnp.float32)
    update = own * (math.sqrt(F) / total_samples)
    lane_of = lax.broadcasted_iota(jnp.int32, (K, 128), 1)
    stats = jnp.zeros((K, 128), jnp.float32)
    for lane, value in enumerate((current * current, current * update, update * update)):
        column = jnp.sum(value, axis=1, keepdims=True)
        stats = jnp.where(lane_of == lane, column, stats)
    stats = jnp.concatenate([stats, jnp.zeros_like(stats)], axis=0).T[:8]

    def total_over(stage, slots, me, count, device_of, value):
        slots[me] = value
        for i in sorted(range(1, count), key=lambda i: -min(i, count - i)):
            pltpu.make_async_remote_copy(
                src_ref=slots.at[me],
                dst_ref=slots.at[me],
                send_sem=stat_send.at[stage],
                recv_sem=stat_recv.at[stage],
                device_id=device_of(i),
                device_id_type=MESH,
            ).start()
        others = slots.at[pl.ds(0, count - 1)]
        pltpu.make_async_copy(others, others, stat_recv.at[stage]).wait()
        total = slots[0]
        for i in range(1, count):
            total = total + slots[i]
        return total

    stats = total_over(0, stat_z, z, NZ, lambda i: (peer(0, i), feat), stats)
    stats = total_over(1, stat_y, y, NY, lambda i: (peer(i, 0), feat), stats)
    stats = total_over(2, stat_f, feat, NF, lambda i: (dp, feat_peer(i)), stats)

    columns = jnp.concatenate([stats, jnp.zeros((120, 128), jnp.float32)], axis=0).T[:K]
    columns = columns * (1.0 / F)
    alignment = columns[:, 1:2]
    keep = 1.0 - STEP * alignment
    squares = (
        keep * keep * columns[:, 0:1]
        + 2.0 * STEP * keep * alignment
        + STEP * STEP * columns[:, 2:3]
    )
    scale = lax.rsqrt(jnp.maximum(squares, 0.0) + EPSILON)
    o_ref[...] = ((keep * current + STEP * update) * scale).astype(jnp.bfloat16)

    sent = gathered.at[pl.ds(0, COPIES)]
    pltpu.make_async_copy(sent, sent, gather_send).wait()
    pltpu.make_async_copy(seven, seven, score_send).wait()
    pltpu.make_async_copy(sent, sent, scatter_send).wait()
    for stage, (slots, count) in enumerate(((stat_z, NZ), (stat_y, NY), (stat_f, NF))):
        others = slots.at[pl.ds(0, count - 1)]
        pltpu.make_async_copy(others, others, stat_send.at[stage]).wait()


def shards(samples, estimates):
    shaped = estimates.reshape(K, WIDTH)
    total_samples = samples.shape[0] * lax.axis_size("dp")
    bf16, f32 = jnp.bfloat16, jnp.float32
    dma = pltpu.SemaphoreType.DMA
    updated = pl.pallas_call(
        functools.partial(kernel, total_samples),
        out_shape=jax.ShapeDtypeStruct((K, WIDTH), bf16),
        in_specs=[
            pl.BlockSpec(memory_space=pl.ANY),
            pl.BlockSpec(memory_space=pl.ANY),
        ],
        out_specs=pl.BlockSpec(memory_space=pltpu.VMEM),
        scratch_shapes=[
            pltpu.VMEM((ROWS, NY * NZ * WIDTH), bf16),
            pltpu.VMEM((K, WIDTH), bf16),
            pltpu.VMEM((NY * NZ, K, WIDTH), bf16),
            pltpu.VMEM((NF, K, ROWS), bf16),
            pltpu.VMEM((COPIES, K, WIDTH), bf16),
            pltpu.VMEM((COPIES, K, WIDTH), bf16),
            pltpu.VMEM((NZ, 8, 128), f32),
            pltpu.VMEM((NY, 8, 128), f32),
            pltpu.VMEM((NF, 8, 128), f32),
            dma,
            dma,
            dma,
            dma((COPIES,)),
            dma,
            dma,
            dma,
            dma((COPIES,)),
            dma((3,)),
            dma((3,)),
        ],
        compiler_params=pltpu.CompilerParams(
            collective_id=0,
            has_side_effects=True,
            vmem_limit_bytes=60 * 1024 * 1024,
        ),
        cost_estimate=pl.CostEstimate(
            flops=4 * K * ROWS * NY * NZ * WIDTH,
            bytes_accessed=2 * ROWS * NY * NZ * WIDTH,
            transcendentals=0,
        ),
    )(samples, shaped)
    return updated.reshape(K, 1, WIDTH)


def solution(mesh):
    return jax.shard_map(
        shards,
        mesh=mesh,
        in_specs=(P("dp", "feat"), P(None, "feat", "dp")),
        out_specs=P(None, "feat", "dp"),
        check_vma=False,
    )
```

time: 100 us -> 81.6 us (0.82)
  Pallas kernels: 98.9 us -> 80.1 us
    pallas_call x1, Pallas kernels: 98.9 us -> 80.1 us  [shards(): pl.pallas_call(functools.partial(kernel, total_samples), out_shape=jax.Sh...]
where the time goes in v3:
time: 81.6 us; the launch traced here: 81.5 us
  Pallas kernels  80.1 us (98%)
  local copies, waits for them, and re-layouts  1.38 us (2%)
    pallas_call x1, Pallas kernels, shards(): pl.pallas_call(functools.partial(kernel, total_samples), out_shape=jax.Sh...  80.1 us

profile of v3, /device:TPU:1, one launch (start us, length us, event | category | flops | bytes accessed | tf_op | source)
XLA Modules:
  0.0 81.5 jit_solution(11043652040451087447)
XLA Ops:
  0.0 80.1 %shard_map.28 = bf16[64,256]{1,0:T(8,128)(2,1)} custom-call(bf16[128,16384]{1,0:T(8,128)(2,1)} %x_hbm.1, bf16[64,256]{1,0:T(8,128)(2,1)} %bitcast.3), custom_call_target="tpu_custom_call" | custom-call | flops 536870912 | bytes 4194304 | tf_op jit(solution)/shard_map/pallas_call | solution.py:314
  80.1 1.4 %copy.4 = bf16[64,1,256]{2,0,1:T(8,128)(2,1)} copy(bf16[64,1,256]{2,0,1:T(8,128)(2,1)} %bitcast.2) | data formatting | bytes 65536

commit v4 on v3

--- a/solution.py
+++ b/solution.py
@@ -13,7 +13,7 @@
 EPSILON = 1e-06
 MESH = pl.DeviceIdType.MESH
 GROUP = 2
-AHEAD = 2
+AHEAD = 3
 ROOT = (0, 0)
 
 NY, NZ, NF = 4, 16, 8
@@ -22,53 +22,95 @@
 WIDTH = 256
 
 ARRIVALS = (
-    (-1, 0), (1, 0), (0, 3), (0, -3), (2, 0), (0, 1), (0, -1), (-1, 1),
-    (-1, -1), (1, -1), (-1, 3), (1, 3), (-1, -3), (1, -3), (0, 6), (2, 1),
-    (1, 1), (0, -6), (0, 4), (2, -1), (0, -4), (0, -2), (2, 3), (-1, -2),
-    (2, -3), (-1, 4), (-1, 2), (1, -2), (-1, -6), (2, 6), (0, 5), (0, 7),
-    (-1, -4), (1, 6), (0, -7), (1, 2), (2, -2), (1, -6), (2, -4), (0, -5),
-    (2, 2), (1, 4), (-1, -7), (2, 7), (2, -6), (0, 2), (2, 5), (1, 7),
-    (-1, 5), (-1, 6), (0, 8), (1, -5), (1, -4), (1, -7), (2, -5), (-1, -5),
-    (2, 4), (2, 8), (-1, 8), (1, 5), (-1, 7), (1, 8), (2, -7),
+    (-1, 0), (0, -2), (1, 0), (2, 0), (0, 3), (0, 1), (0, -3), (-1, 1),
+    (0, -1), (-1, -2), (1, -2), (1, 3), (-1, 3), (1, 1), (-1, -3), (0, -6),
+    (1, -3), (2, 1), (0, 2), (0, 7), (0, -4), (1, -1), (0, 4), (2, -1),
+    (1, 2), (2, 3), (-1, -1), (-1, 2), (2, -2), (1, 5), (0, -7), (2, -3),
+    (-1, 4), (1, -6), (1, -4), (2, -6), (0, 8), (0, 6), (-1, -6), (0, 5),
+    (1, 7), (0, -5), (2, 7), (2, 4), (2, 2), (1, 4), (-1, 7), (1, 6),
+    (2, 5), (2, -4), (-1, -4), (-1, 5), (1, -7), (2, -7), (-1, 8), (2, -5),
+    (1, 8), (-1, -7), (-1, 6), (-1, -5), (1, -5), (2, 6), (2, 8),
 )
 TARGETS = {
-    (0, 0): ((0, 3), (0, -3), (-1, 0), (0, 1), (1, 0), (2, 0), (0, -1)),
-    (-1, 0): ((-1, -1), (-1, 1)),
-    (1, 0): ((1, -1),),
-    (0, 3): ((0, 6), (0, 4), (-1, 3), (1, 3)),
-    (0, -3): ((0, -6), (-1, -3), (0, -4), (1, -3), (0, -2)),
+    (-1, -6): ((-1, -7), (-1, -5)),
+    (-1, -3): ((2, -3),),
+    (-1, -2): ((2, -2),),
+    (-1, 0): ((-1, 1),),
+    (-1, 1): ((2, 1),),
+    (-1, 3): ((-1, 4), (-1, 2)),
+    (-1, 4): ((-1, 5),),
+    (0, -7): ((1, -7),),
+    (0, -6): ((2, -6), (-1, -6), (0, -7), (1, -6)),
+    (0, -5): ((1, -5),),
+    (0, -4): ((0, -5), (-1, -4)),
+    (0, -3): ((-1, -3), (0, -4), (1, -3)),
+    (0, -2): ((0, -6), (0, -1), (-1, -2), (1, -2)),
+    (0, -1): ((2, -1), (-1, -1), (1, -1)),
+    (0, 0): ((0, 3), (0, -2), (0, -3), (-1, 0), (0, 1), (2, 0), (1, 0)),
     (0, 1): ((1, 1),),
-    (-1, 1): ((2, 1),),
-    (-1, -1): ((-1, -2), (2, -1)),
-    (-1, 3): ((-1, 2), (-1, 4)),
-    (1, 3): ((2, 3),),
+    (0, 3): ((0, 7), (1, 3), (-1, 3), (0, 4), (0, 2)),
+    (0, 4): ((0, 5),),
+    (0, 6): ((-1, 6),),
+    (0, 7): ((2, 7), (0, 6), (0, 8), (-1, 7), (1, 7)),
+    (0, 8): ((-1, 8), (1, 8)),
+    (1, -3): ((1, -4),),
+    (1, 2): ((2, 2),),
+    (1, 3): ((1, 5), (1, 2), (2, 3)),
+    (1, 5): ((1, 4), (1, 6), (2, 5)),
+    (2, -6): ((2, -7), (2, -5)),
+    (2, -3): ((2, -4),),
+    (2, 3): ((2, 4),),
+    (2, 7): ((2, 6), (2, 8)),
+}
+DEPARTURES = (
+    (2, 6), (-1, 7), (2, 8), (-1, 8), (1, 8), (2, -7), (1, 7), (2, -6),
+    (2, 4), (-1, -6), (1, 4), (1, 6), (2, -5), (2, -3), (1, -3), (2, -2),
+    (2, 7), (-1, 6), (2, 2), (-1, -7), (0, 7), (0, 8), (0, -6), (1, -5),
+    (1, -7), (1, 5), (1, -6), (-1, -5), (1, 2), (2, -4), (-1, 4), (0, 6),
+    (2, 5), (2, 3), (-1, 5), (-1, -3), (0, -7), (-1, -2), (-1, 2), (1, -2),
+    (2, 1), (-1, -4), (0, -5), (1, -4), (0, 2), (0, 4), (2, -1), (0, 5),
+    (0, -3), (-1, 3), (1, 3), (-1, -1), (-1, 1), (0, -2), (1, -1), (1, 1),
+    (2, 0), (0, -4), (0, 1), (0, 3), (-1, 0), (0, -1), (1, 0),
+)
+PARTS = {
+    (2, 7): ((2, 6),),
+    (-1, 6): ((-1, 7),),
+    (-1, -7): ((-1, 8),),
+    (0, 8): ((2, 8),),
+    (1, -7): ((1, 8), (2, -7)),
+    (1, 5): ((1, 7),),
+    (1, -6): ((2, -6),),
+    (-1, -5): ((-1, -6),),
+    (2, -4): ((2, -5),),
+    (-1, 4): ((1, 4),),
+    (0, 6): ((1, 6),),
+    (2, 5): ((2, 4), (2, 7)),
+    (-1, 5): ((-1, 6),),
     (-1, -3): ((2, -3),),
-    (1, -3): ((1, -2),),
-    (0, 6): ((2, 6), (1, 6), (0, 5), (0, 7)),
-    (1, 1): ((1, 2),),
-    (0, -6): ((-1, -6), (0, -5), (0, -7), (1, -6)),
-    (0, 4): ((1, 4),),
-    (0, -4): ((-1, -4),),
-    (-1, -2): ((2, -2),),
-    (2, -3): ((2, -4),),
-    (-1, 2): ((0, 2), (2, 2)),
-    (-1, -6): ((2, -6), (-1, -7)),
-    (2, 6): ((2, 5), (2, 7), (-1, 6)),
-    (0, 5): ((-1, 5),),
-    (1, 6): ((1, 7),),
-    (0, -7): ((0, 8), (1, -7)),
-    (1, -6): ((1, -5),),
-    (2, -4): ((2, -5), (1, -4)),
-    (0, -5): ((-1, -5),),
-    (1, 4): ((2, 4),),
-    (-1, -7): ((-1, 8),),
-    (2, 7): ((2, 8), (-1, 7)),
-    (2, -6): ((2, -7),),
-    (2, 5): ((1, 5),),
-    (1, 7): ((1, 8),),
+    (0, -7): ((-1, -7), (0, 8), (1, -7)),
+    (-1, 2): ((2, 2),),
+    (1, -2): ((1, -3), (2, -2)),
+    (-1, -4): ((2, -4),),
+    (0, -5): ((0, -6), (-1, -5)),
+    (1, -4): ((1, -5), (1, -6)),
+    (0, 5): ((0, 7), (1, 5), (0, 6), (2, 5)),
+    (0, -3): ((-1, -3),),
+    (-1, 3): ((-1, 4), (-1, 5)),
+    (1, 3): ((1, 2), (2, 3)),
+    (-1, 1): ((-1, 2),),
+    (0, -2): ((-1, -2), (1, -2)),
+    (2, 0): ((2, 1),),
+    (0, -4): ((0, -7), (-1, -4), (0, -5), (1, -4)),
+    (0, 3): ((0, 2), (0, 4), (0, 5), (-1, 3), (1, 3)),
+    (-1, 0): ((-1, 1),),
+    (0, -1): ((2, -1), (0, -3), (-1, -1), (0, -2), (1, -1)),
+    (1, 0): ((1, 1), (2, 0)),
+    (0, 0): ((0, -4), (0, 1), (0, 3), (-1, 0), (0, -1), (1, 0)),
 }
-NUMBER = {node: i for i, node in enumerate(ARRIVALS)}
 COPIES = len(ARRIVALS)
+ARRIVAL = {node: i for i, node in enumerate(ARRIVALS)}
+DEPARTURE = {node: i for i, node in enumerate(DEPARTURES)}
+JOINS = {part: node for node, parts in PARTS.items() for part in parts}
 
 
 def minus(a, b):
@@ -79,7 +121,8 @@
 MOVES = sorted(
     {
         way
-        for node, targets in TARGETS.items()
+        for tree in (TARGETS, PARTS)
+        for node, targets in tree.items()
         for target in targets
         for way in (minus(target, node), minus(node, target))
     }
@@ -98,8 +141,7 @@
     scatter_out,
     scatter_in,
     stat_z,
-    stat_y,
-    stat_f,
+    stat_g,
     x_sem,
     u_sem,
     gather_send,
@@ -116,8 +158,10 @@
     y = lax.div(dp, NZ)
     z = lax.rem(dp, NZ)
 
+    way = 1 - 2 * lax.rem(feat, 2)
+
     def peer(dy, dz):
-        return lax.rem(y + (dy + NY), NY) * NZ + lax.rem(z + (dz + NZ), NZ)
+        return lax.rem(y + way * dy + NY, NY) * NZ + lax.rem(z + way * dz + NZ, NZ)
 
     def origin(node):
         return peer(-node[0], -node[1])
@@ -131,7 +175,7 @@
     x_copy.start()
 
     barrier = pltpu.get_barrier_semaphore()
-    partners = [(peer(*way), feat) for way in MOVES]
+    partners = [(peer(*move), feat) for move in MOVES]
     partners += [(dp, feat_peer(i)) for i in range(1, NF)]
     for partner in partners:
         pl.semaphore_signal(barrier, inc=1, device_id=partner, device_id_type=MESH)
@@ -144,14 +188,14 @@
             src_ref=gathered.at[index] if src is None else src,
             dst_ref=gathered.at[index],
             send_sem=gather_send,
-            recv_sem=gather_recv.at[NUMBER[target]],
+            recv_sem=gather_recv.at[ARRIVAL[target]],
             device_id=(peer(*minus(target, node)), feat),
             device_id_type=MESH,
         )
 
     def arrived(node):
         shard = gathered.at[origin(node)]
-        pltpu.make_async_copy(shard, shard, gather_recv.at[NUMBER[node]]).wait()
+        pltpu.make_async_copy(shard, shard, gather_recv.at[ARRIVAL[node]]).wait()
 
     for target in TARGETS[ROOT]:
         gather_copy(ROOT, target, u_ref).start()
@@ -222,36 +266,35 @@
             preferred_element_type=jnp.float32,
         )
 
-    def scatter_copy(node, target):
-        slot = NUMBER[target]
+    def scatter_copy(node):
+        slot = DEPARTURE[node]
         return pltpu.make_async_remote_copy(
             src_ref=scatter_out.at[slot],
             dst_ref=scatter_in.at[slot],
             send_sem=scatter_send,
             recv_sem=scatter_recv.at[slot],
-            device_id=(peer(*minus(node, target)), feat),
+            device_id=(peer(*minus(JOINS[node], node)), feat),
             device_id_type=MESH,
         )
 
     def take(total, node):
-        for target in reversed(TARGETS.get(node, ())):
-            slot = NUMBER[target]
+        for part in PARTS.get(node, ()):
+            slot = DEPARTURE[part]
             pltpu.make_async_copy(
                 scatter_in.at[slot], scatter_in.at[slot], scatter_recv.at[slot]
             ).wait()
             total = total + scatter_in[slot].astype(jnp.float32)
         return total
 
-    sources = {target: node for node, targets in TARGETS.items() for target in targets}
-    departures = ARRIVALS[::-1] + (ROOT,)
-    terms = [term(node) for node in departures[:AHEAD]]
-    for i, node in enumerate(departures):
-        if i + AHEAD < len(departures):
-            terms.append(term(departures[i + AHEAD]))
+    stops = DEPARTURES + (ROOT,)
+    terms = [term(node) for node in stops[:AHEAD]]
+    for i, node in enumerate(stops):
+        if i + AHEAD < len(stops):
+            terms.append(term(stops[i + AHEAD]))
         total = take(terms.pop(0), node)
         if node != ROOT:
-            scatter_out[NUMBER[node]] = total.astype(jnp.bfloat16)
-            scatter_copy(sources[node], node).start()
+            scatter_out[DEPARTURE[node]] = total.astype(jnp.bfloat16)
+            scatter_copy(node).start()
     own = total
 
     current = u_ref[...].astype(jnp.float32)
@@ -263,9 +306,12 @@
         stats = jnp.where(lane_of == lane, column, stats)
     stats = jnp.concatenate([stats, jnp.zeros_like(stats)], axis=0).T[:8]
 
-    def total_over(stage, slots, me, count, device_of, value):
+    def ring(i, count):
+        return min(i, count - i)
+
+    def total_over(stage, slots, me, count, device_of, distance, value):
         slots[me] = value
-        for i in sorted(range(1, count), key=lambda i: -min(i, count - i)):
+        for i in sorted(range(1, count), key=distance, reverse=True):
             pltpu.make_async_remote_copy(
                 src_ref=slots.at[me],
                 dst_ref=slots.at[me],
@@ -281,9 +327,14 @@
             total = total + slots[i]
         return total
 
-    stats = total_over(0, stat_z, z, NZ, lambda i: (peer(0, i), feat), stats)
-    stats = total_over(1, stat_y, y, NY, lambda i: (peer(i, 0), feat), stats)
-    stats = total_over(2, stat_f, feat, NF, lambda i: (dp, feat_peer(i)), stats)
+    def group(i):
+        return (peer(i // NF, 0), feat_peer(i % NF))
+
+    def group_distance(i):
+        return 2 * ring(i // NF, NY) + ring(i % NF, NF)
+
+    stats = total_over(1, stat_g, y * NF + feat, NY * NF, group, group_distance, stats)
+    stats = total_over(0, stat_z, z, NZ, lambda i: (peer(0, i), feat), lambda i: ring(i, NZ), stats)
 
     columns = jnp.concatenate([stats, jnp.zeros((120, 128), jnp.float32)], axis=0).T[:K]
     columns = columns * (1.0 / F)
@@ -301,7 +352,7 @@
     pltpu.make_async_copy(sent, sent, gather_send).wait()
     pltpu.make_async_copy(seven, seven, score_send).wait()
     pltpu.make_async_copy(sent, sent, scatter_send).wait()
-    for stage, (slots, count) in enumerate(((stat_z, NZ), (stat_y, NY), (stat_f, NF))):
+    for stage, (slots, count) in enumerate(((stat_z, NZ), (stat_g, NY * NF))):
         others = slots.at[pl.ds(0, count - 1)]
         pltpu.make_async_copy(others, others, stat_send.at[stage]).wait()
 
@@ -327,8 +378,7 @@
             pltpu.VMEM((COPIES, K, WIDTH), bf16),
             pltpu.VMEM((COPIES, K, WIDTH), bf16),
             pltpu.VMEM((NZ, 8, 128), f32),
-            pltpu.VMEM((NY, 8, 128), f32),
-            pltpu.VMEM((NF, 8, 128), f32),
+            pltpu.VMEM((NY * NF, 8, 128), f32),
             dma,
             dma,
             dma,
@@ -337,8 +387,8 @@
             dma,
             dma,
             dma((COPIES,)),
-            dma((3,)),
-            dma((3,)),
+            dma((2,)),
+            dma((2,)),
         ],
         compiler_params=pltpu.CompilerParams(
             collective_id=0,

time: 81.6 us -> 77.2 us (0.946)
  Pallas kernels: 80.1 us -> 75.6 us
    pallas_call x1, Pallas kernels: 80.1 us -> 75.6 us  [shards(): pl.pallas_call(functools.partial(kernel, total_samples), out_shape=jax.Sh...]
where the time goes in v4:
time: 77.2 us; the launch traced here: 77 us
  Pallas kernels  75.6 us (98%)
  local copies, waits for them, and re-layouts  1.38 us (2%)
    pallas_call x1, Pallas kernels, shards(): pl.pallas_call(functools.partial(kernel, total_samples), out_shape=jax.Sh...  75.6 us

profile of v4, /device:TPU:1, one launch (start us, length us, event | category | flops | bytes accessed | tf_op | source)
XLA Modules:
  0.0 77.0 jit_solution(10880553696655266770)
XLA Ops:
  0.0 75.6 %shard_map.28 = bf16[64,256]{1,0:T(8,128)(2,1)} custom-call(bf16[128,16384]{1,0:T(8,128)(2,1)} %x_hbm.1, bf16[64,256]{1,0:T(8,128)(2,1)} %bitcast.3), custom_call_target="tpu_custom_call" | custom-call | flops 536870912 | bytes 4194304 | tf_op jit(solution)/shard_map/pallas_call | solution.py:365
  75.6 1.4 %copy.4 = bf16[64,1,256]{2,0,1:T(8,128)(2,1)} copy(bf16[64,1,256]{2,0,1:T(8,128)(2,1)} %bitcast.2) | data formatting | bytes 65536

commit v5 on v4

--- a/solution.py
+++ b/solution.py
@@ -63,49 +63,54 @@
     (2, 7): ((2, 6), (2, 8)),
 }
 DEPARTURES = (
-    (2, 6), (-1, 7), (2, 8), (-1, 8), (1, 8), (2, -7), (1, 7), (2, -6),
-    (2, 4), (-1, -6), (1, 4), (1, 6), (2, -5), (2, -3), (1, -3), (2, -2),
-    (2, 7), (-1, 6), (2, 2), (-1, -7), (0, 7), (0, 8), (0, -6), (1, -5),
-    (1, -7), (1, 5), (1, -6), (-1, -5), (1, 2), (2, -4), (-1, 4), (0, 6),
-    (2, 5), (2, 3), (-1, 5), (-1, -3), (0, -7), (-1, -2), (-1, 2), (1, -2),
-    (2, 1), (-1, -4), (0, -5), (1, -4), (0, 2), (0, 4), (2, -1), (0, 5),
-    (0, -3), (-1, 3), (1, 3), (-1, -1), (-1, 1), (0, -2), (1, -1), (1, 1),
-    (2, 0), (0, -4), (0, 1), (0, 3), (-1, 0), (0, -1), (1, 0),
+    (2, 8), (2, 7), (0, -3), (0, 1), (2, -3), (1, 8), (2, -7), (-1, -7),
+    (-1, 7), (1, -7), (1, 7), (-1, -6), (-1, 4), (1, 2), (1, 6), (2, -5),
+    (2, 3), (2, 5), (-1, 3), (0, -2), (2, -2), (2, 2), (1, -5), (1, -3),
+    (2, -4), (1, -2), (-1, 8), (2, 6), (0, 2), (-1, -3), (2, -6), (0, -7),
+    (1, -6), (0, 7), (-1, -5), (-1, 5), (1, 3), (0, -5), (1, 5), (2, 4),
+    (0, 8), (0, -1), (-1, 6), (2, -1), (-1, 2), (2, 1), (1, -4), (1, -1),
+    (-1, -2), (0, -6), (-1, -4), (0, 3), (0, 5), (1, 4), (0, 6), (2, 0),
+    (1, 1), (-1, 1), (-1, -1), (0, -4), (0, 4), (1, 0), (-1, 0),
 )
 PARTS = {
-    (2, 7): ((2, 6),),
-    (-1, 6): ((-1, 7),),
-    (-1, -7): ((-1, 8),),
-    (0, 8): ((2, 8),),
-    (1, -7): ((1, 8), (2, -7)),
-    (1, 5): ((1, 7),),
-    (1, -6): ((2, -6),),
-    (-1, -5): ((-1, -6),),
-    (2, -4): ((2, -5),),
-    (-1, 4): ((1, 4),),
-    (0, 6): ((1, 6),),
-    (2, 5): ((2, 4), (2, 7)),
-    (-1, 5): ((-1, 6),),
-    (-1, -3): ((2, -3),),
-    (0, -7): ((-1, -7), (0, 8), (1, -7)),
-    (-1, 2): ((2, 2),),
-    (1, -2): ((1, -3), (2, -2)),
-    (-1, -4): ((2, -4),),
-    (0, -5): ((0, -6), (-1, -5)),
-    (1, -4): ((1, -5), (1, -6)),
-    (0, 5): ((0, 7), (1, 5), (0, 6), (2, 5)),
-    (0, -3): ((-1, -3),),
-    (-1, 3): ((-1, 4), (-1, 5)),
-    (1, 3): ((1, 2), (2, 3)),
+    (-1, 8): ((2, 8),),
+    (2, 6): ((2, 7),),
+    (0, 2): ((0, 1),),
+    (-1, -3): ((0, -3), (2, -3)),
+    (2, -6): ((2, -7),),
+    (0, -7): ((-1, -7),),
+    (1, -6): ((1, -7),),
+    (0, 7): ((1, 7),),
+    (-1, -5): ((-1, -6), (2, -5)),
+    (-1, 5): ((-1, 4),),
+    (1, 3): ((1, 2),),
+    (0, -5): ((1, -5),),
+    (1, 5): ((1, 6), (2, 5)),
+    (2, 4): ((2, 3),),
+    (0, 8): ((1, 8), (-1, 8)),
+    (0, -1): ((0, -2),),
+    (-1, 6): ((-1, 7), (2, 6)),
+    (2, -1): ((2, -2),),
+    (-1, 2): ((-1, 3), (0, 2)),
+    (2, 1): ((2, 2),),
+    (1, -4): ((1, -3), (2, -4)),
+    (1, -1): ((1, -2),),
+    (-1, -2): ((-1, -3),),
+    (0, -6): ((2, -6), (0, -7), (1, -6)),
+    (-1, -4): ((-1, -5),),
+    (0, 3): ((1, 3),),
+    (0, 5): ((-1, 5), (1, 5)),
+    (1, 4): ((2, 4),),
+    (0, 6): ((0, 7), (0, 8), (-1, 6)),
+    (2, 0): ((2, -1),),
+    (1, 1): ((2, 1),),
     (-1, 1): ((-1, 2),),
-    (0, -2): ((-1, -2), (1, -2)),
-    (2, 0): ((2, 1),),
-    (0, -4): ((0, -7), (-1, -4), (0, -5), (1, -4)),
-    (0, 3): ((0, 2), (0, 4), (0, 5), (-1, 3), (1, 3)),
-    (-1, 0): ((-1, 1),),
-    (0, -1): ((2, -1), (0, -3), (-1, -1), (0, -2), (1, -1)),
-    (1, 0): ((1, 1), (2, 0)),
-    (0, 0): ((0, -4), (0, 1), (0, 3), (-1, 0), (0, -1), (1, 0)),
+    (-1, -1): ((0, -1), (-1, -2)),
+    (0, -4): ((0, -5), (1, -4), (0, -6), (-1, -4)),
+    (0, 4): ((0, 3), (0, 5), (1, 4), (0, 6)),
+    (1, 0): ((1, -1), (2, 0), (1, 1)),
+    (-1, 0): ((-1, 1), (-1, -1)),
+    (0, 0): ((0, -4), (0, 4), (1, 0), (-1, 0)),
 }
 COPIES = len(ARRIVALS)
 ARRIVAL = {node: i for i, node in enumerate(ARRIVALS)}
@@ -160,11 +165,11 @@
 
     way = 1 - 2 * lax.rem(feat, 2)
 
-    def peer(dy, dz):
+    def peer(dy, dz, way=way):
         return lax.rem(y + way * dy + NY, NY) * NZ + lax.rem(z + way * dz + NZ, NZ)
 
-    def origin(node):
-        return peer(-node[0], -node[1])
+    def origin(node, way=way):
+        return peer(-node[0], -node[1], way)
 
     def feat_peer(i):
         return lax.rem(feat + i, NF)
@@ -183,18 +188,18 @@
     pl.semaphore_wait(barrier, len(partners))
 
     def gather_copy(node, target, src=None):
-        index = origin(node)
+        index = origin(node, 1)
         return pltpu.make_async_remote_copy(
             src_ref=gathered.at[index] if src is None else src,
             dst_ref=gathered.at[index],
             send_sem=gather_send,
             recv_sem=gather_recv.at[ARRIVAL[target]],
-            device_id=(peer(*minus(target, node)), feat),
+            device_id=(peer(*minus(target, node), 1), feat),
             device_id_type=MESH,
         )
 
     def arrived(node):
-        shard = gathered.at[origin(node)]
+        shard = gathered.at[origin(node, 1)]
         pltpu.make_async_copy(shard, shard, gather_recv.at[ARRIVAL[node]]).wait()
 
     for target in TARGETS[ROOT]:
@@ -206,7 +211,7 @@
 
     def partial_scores(acc, nodes):
         for node in nodes:
-            index = origin(node)
+            index = origin(node, 1)
             acc = acc + lax.dot_general(
                 gathered[index],
                 x_v[:, columns_of(index)],
@@ -300,11 +305,21 @@
     current = u_ref[...].astype(jnp.float32)
     update = own * (math.sqrt(F) / total_samples)
     lane_of = lax.broadcasted_iota(jnp.int32, (K, 128), 1)
-    stats = jnp.zeros((K, 128), jnp.float32)
-    for lane, value in enumerate((current * current, current * update, update * update)):
-        column = jnp.sum(value, axis=1, keepdims=True)
-        stats = jnp.where(lane_of == lane, column, stats)
-    stats = jnp.concatenate([stats, jnp.zeros_like(stats)], axis=0).T[:8]
+
+    def row_sum(value):
+        return jnp.sum(value, axis=1, keepdims=True)
+
+    stats = jnp.concatenate(
+        [
+            jnp.where(
+                lane_of == 0,
+                row_sum(current * current),
+                jnp.where(lane_of == 1, row_sum(update * update), 0.0),
+            ),
+            jnp.where(lane_of == 0, row_sum(current * update), 0.0),
+        ],
+        axis=0,
+    ).T[:2]
 
     def ring(i, count):
         return min(i, count - i)
@@ -336,14 +351,16 @@
     stats = total_over(1, stat_g, y * NF + feat, NY * NF, group, group_distance, stats)
     stats = total_over(0, stat_z, z, NZ, lambda i: (peer(0, i), feat), lambda i: ring(i, NZ), stats)
 
-    columns = jnp.concatenate([stats, jnp.zeros((120, 128), jnp.float32)], axis=0).T[:K]
+    row_of = lax.broadcasted_iota(jnp.int32, (8, 128), 0)
+    rows = jnp.where(row_of == 0, stats[0:1], jnp.where(row_of == 1, stats[1:2], 0.0))
+    columns = jnp.concatenate([rows, jnp.zeros((120, 128), jnp.float32)], axis=0).T
     columns = columns * (1.0 / F)
-    alignment = columns[:, 1:2]
+    alignment = columns[K:, 0:1]
     keep = 1.0 - STEP * alignment
     squares = (
-        keep * keep * columns[:, 0:1]
+        keep * keep * columns[:K, 0:1]
         + 2.0 * STEP * keep * alignment
-        + STEP * STEP * columns[:, 2:3]
+        + STEP * STEP * columns[:K, 1:2]
     )
     scale = lax.rsqrt(jnp.maximum(squares, 0.0) + EPSILON)
     o_ref[...] = ((keep * current + STEP * update) * scale).astype(jnp.bfloat16)
@@ -377,8 +394,8 @@
             pltpu.VMEM((NF, K, ROWS), bf16),
             pltpu.VMEM((COPIES, K, WIDTH), bf16),
             pltpu.VMEM((COPIES, K, WIDTH), bf16),
-            pltpu.VMEM((NZ, 8, 128), f32),
-            pltpu.VMEM((NY * NF, 8, 128), f32),
+            pltpu.VMEM((NZ, 2, 128), f32),
+            pltpu.VMEM((NY * NF, 2, 128), f32),
             dma,
             dma,
             dma,

time: 77.2 us -> 75.3 us (0.975)
  Pallas kernels: 75.6 us -> 73.8 us
    pallas_call x1, Pallas kernels: 75.6 us -> 73.8 us  [shards(): pl.pallas_call(functools.partial(kernel, total_samples), out_shape=jax.Sh...]
where the time goes in v5:
time: 75.3 us; the launch traced here: 75.1 us
  Pallas kernels  73.8 us (98%)
  local copies, waits for them, and re-layouts  1.38 us (2%)
    pallas_call x1, Pallas kernels, shards(): pl.pallas_call(functools.partial(kernel, total_samples), out_shape=jax.Sh...  73.8 us

profile of v5, /device:TPU:1, one launch (start us, length us, event | category | flops | bytes accessed | tf_op | source)
XLA Modules:
  0.0 75.1 jit_solution(13693938552808086855)
XLA Ops:
  0.0 73.8 %shard_map.28 = bf16[64,256]{1,0:T(8,128)(2,1)} custom-call(bf16[128,16384]{1,0:T(8,128)(2,1)} %x_hbm.1, bf16[64,256]{1,0:T(8,128)(2,1)} %bitcast.3), custom_call_target="tpu_custom_call" | custom-call | flops 536870912 | bytes 4194304 | tf_op jit(solution)/shard_map/pallas_call | solution.py:382
  73.8 1.4 %copy.4 = bf16[64,1,256]{2,0,1:T(8,128)(2,1)} copy(bf16[64,1,256]{2,0,1:T(8,128)(2,1)} %bitcast.2) | data formatting | bytes 65536

commit v6 on v5

--- a/solution.py
+++ b/solution.py
@@ -22,44 +22,45 @@
 WIDTH = 256
 
 ARRIVALS = (
-    (-1, 0), (0, -2), (1, 0), (2, 0), (0, 3), (0, 1), (0, -3), (-1, 1),
-    (0, -1), (-1, -2), (1, -2), (1, 3), (-1, 3), (1, 1), (-1, -3), (0, -6),
-    (1, -3), (2, 1), (0, 2), (0, 7), (0, -4), (1, -1), (0, 4), (2, -1),
-    (1, 2), (2, 3), (-1, -1), (-1, 2), (2, -2), (1, 5), (0, -7), (2, -3),
-    (-1, 4), (1, -6), (1, -4), (2, -6), (0, 8), (0, 6), (-1, -6), (0, 5),
-    (1, 7), (0, -5), (2, 7), (2, 4), (2, 2), (1, 4), (-1, 7), (1, 6),
-    (2, 5), (2, -4), (-1, -4), (-1, 5), (1, -7), (2, -7), (-1, 8), (2, -5),
-    (1, 8), (-1, -7), (-1, 6), (-1, -5), (1, -5), (2, 6), (2, 8),
+    (-1, 0), (1, 0), (2, 0), (0, 4), (0, -4), (0, 1), (-1, -2), (-1, -1),
+    (2, 2), (2, -1), (-1, 4), (1, 4), (0, 3), (-1, -4), (1, -4), (-1, 1),
+    (1, 1), (0, 7), (0, -6), (2, -2), (0, -2), (0, 5), (0, -5), (1, 2),
+    (-1, 2), (0, 2), (-1, -3), (1, -1), (2, 4), (-1, 5), (1, 3), (-1, 3),
+    (2, -4), (1, 5), (2, 1), (1, -3), (1, 7), (2, 7), (0, 8), (1, -6),
+    (-1, -7), (-1, 7), (0, 6), (1, -2), (-1, -6), (-1, -5), (-1, 6), (2, 3),
+    (0, -7), (0, -1), (1, 6), (2, 5), (0, -3), (2, -5), (1, 8), (2, -3),
+    (2, 6), (-1, 8), (2, 8), (2, -6), (1, -7), (2, -7), (1, -5),
 )
 TARGETS = {
-    (-1, -6): ((-1, -7), (-1, -5)),
-    (-1, -3): ((2, -3),),
-    (-1, -2): ((2, -2),),
-    (-1, 0): ((-1, 1),),
+    (-1, -7): ((2, -7),),
+    (-1, -4): ((-1, -7), (-1, -5)),
+    (-1, -2): ((0, -2), (-1, -3), (2, -2)),
+    (-1, 0): ((-1, -2), (-1, -1)),
     (-1, 1): ((2, 1),),
-    (-1, 3): ((-1, 4), (-1, 2)),
     (-1, 4): ((-1, 5),),
-    (0, -7): ((1, -7),),
-    (0, -6): ((2, -6), (-1, -6), (0, -7), (1, -6)),
-    (0, -5): ((1, -5),),
-    (0, -4): ((0, -5), (-1, -4)),
-    (0, -3): ((-1, -3), (0, -4), (1, -3)),
-    (0, -2): ((0, -6), (0, -1), (-1, -2), (1, -2)),
-    (0, -1): ((2, -1), (-1, -1), (1, -1)),
-    (0, 0): ((0, 3), (0, -2), (0, -3), (-1, 0), (0, 1), (2, 0), (1, 0)),
-    (0, 1): ((1, 1),),
-    (0, 3): ((0, 7), (1, 3), (-1, 3), (0, 4), (0, 2)),
-    (0, 4): ((0, 5),),
-    (0, 6): ((-1, 6),),
-    (0, 7): ((2, 7), (0, 6), (0, 8), (-1, 7), (1, 7)),
-    (0, 8): ((-1, 8), (1, 8)),
-    (1, -3): ((1, -4),),
-    (1, 2): ((2, 2),),
-    (1, 3): ((1, 5), (1, 2), (2, 3)),
-    (1, 5): ((1, 4), (1, 6), (2, 5)),
-    (2, -6): ((2, -7), (2, -5)),
-    (2, -3): ((2, -4),),
-    (2, 3): ((2, 4),),
+    (-1, 5): ((-1, 6),),
+    (0, -6): ((1, -6), (-1, -6), (0, -7)),
+    (0, -4): ((-1, -4), (0, -6), (1, -4), (0, -5)),
+    (0, -2): ((1, -2),),
+    (0, 0): ((0, 4), (0, -4), (-1, 0), (2, 0), (0, 1), (1, 0)),
+    (0, 1): ((-1, 1), (0, 2), (1, 1)),
+    (0, 3): ((-1, 3),),
+    (0, 4): ((0, 7), (-1, 4), (1, 4), (0, 3), (0, 5)),
+    (0, 5): ((0, 6),),
+    (0, 7): ((2, 7), (0, 8), (1, 7), (-1, 7)),
+    (0, 8): ((-1, 8),),
+    (1, -6): ((1, -7), (1, -5), (2, -6)),
+    (1, -4): ((1, -3), (2, -4)),
+    (1, -3): ((0, -3), (2, -3)),
+    (1, -1): ((0, -1),),
+    (1, 3): ((2, 3),),
+    (1, 4): ((1, 3), (1, 5), (2, 4)),
+    (1, 5): ((1, 6), (2, 5)),
+    (1, 7): ((1, 8),),
+    (2, -4): ((2, -5),),
+    (2, -1): ((1, -1),),
+    (2, 0): ((2, -1), (2, 2)),
+    (2, 2): ((-1, 2), (1, 2)),
     (2, 7): ((2, 6), (2, 8)),
 }
 DEPARTURES = (
@@ -242,7 +243,7 @@
             device_id_type=MESH,
         )
 
-    for i in range(1, NF):
+    for i in (4, 3, 5, 2, 6, 1, 7):
         score_copy(i).start()
     seven = score_slots.at[pl.ds(0, NF - 1)]
     pltpu.make_async_copy(seven, seven, score_recv).wait()

time: 75.3 us -> 75 us (level)
  no operation moved by 1% of the time
where the time goes in v6:
time: 75 us; the launch traced here: 74.9 us
  Pallas kernels  73.5 us (98%)
  local copies, waits for them, and re-layouts  1.38 us (2%)
    pallas_call x1, Pallas kernels, shards(): pl.pallas_call(functools.partial(kernel, total_samples), out_shape=jax.Sh...  73.5 us

profile of v6, /device:TPU:1, one launch (start us, length us, event | category | flops | bytes accessed | tf_op | source)
XLA Modules:
  0.0 74.9 jit_solution(17587725540352120307)
XLA Ops:
  0.0 73.5 %shard_map.28 = bf16[64,256]{1,0:T(8,128)(2,1)} custom-call(bf16[128,16384]{1,0:T(8,128)(2,1)} %x_hbm.1, bf16[64,256]{1,0:T(8,128)(2,1)} %bitcast.3), custom_call_target="tpu_custom_call" | custom-call | flops 536870912 | bytes 4194304 | tf_op jit(solution)/shard_map/pallas_call | solution.py:383
  73.5 1.4 %copy.4 = bf16[64,1,256]{2,0,1:T(8,128)(2,1)} copy(bf16[64,1,256]{2,0,1:T(8,128)(2,1)} %bitcast.2) | data formatting | bytes 65536
